TPU v7x, 32 devices: a whole 2x2x4 slice. The times are simulated.
32 devices in a mesh: group: 1, ep: 32 (over z, y, x, core).
Axes of the slice: x: 2, y: 2, z: 4, core: 2. Of those that a mesh axis runs over, the one named last changes fastest.
Arguments:
- queries: bfloat16 [128, 2, 128, 576], P(('group', 'ep')), may hold values from -16 to 16
- cache_pool: bfloat16 [2176, 64, 576], P(('group', 'ep')), may hold values from -16 to 16
- mig_block: int32 [32, 32], P(('group', 'ep')), may hold values from 0 to 68, as said below
- block_table: int32 [128, 17], P(('group', 'ep')), may hold values from 0 to 99, as said below
- lengths: int32 [128], P(('group', 'ep')), may hold values from 2 to 1088
- hidden_states: bfloat16 [256, 3584], P(('group', 'ep')), may hold values from -6 to 6
- routes: int32 [256, 2], P(('group', 'ep')), may hold values from 0 to 3, all different within a row; in each aligned block of 8 rows (0 to 7, 8 to 15, ...) at most 4 rows name the same one
- route_weight: bfloat16 [256, 2], P(('group', 'ep')), may hold values from 0.19921875 to 1
- w_gate: bfloat16 [32, 3584, 256], P('ep'), may hold values from -0.09375 to 0.09375
- w_up: bfloat16 [32, 3584, 256], P('ep'), may hold values from -0.09375 to 0.09375
- w_down: bfloat16 [32, 256, 3584], P('ep'), may hold values from -0.125 to 0.125
Outputs:
- attn_out: bfloat16 [128, 2, 128, 512], P(('group', 'ep'))
- moe_out: bfloat16 [256, 3584], P(('group', 'ep'))
Inputs may be any that keep to these rules, and one draw needn't show every extreme that they name: `mig_block`: row s names, for each device d that receives a block from device s, the block of s that moves to d; every other entry, always including d = s, is 68; the blocks named in a row differ, and a row names at most 31 of them. `block_table`: entries below 68 name blocks that the request's device keeps (none that it sends away); 68 + s names the block that device s sends to it. On each device every kept block and every arriving block stands exactly once in its requests' tables, and each request's first entry is a kept block. `routes`: A token's 2 experts differ, and the rows of one device name every expert exactly 4 times.
All inputs are finite; a program needn't handle non-finite values.
Results may differ from a plain program's by a relative error of at most 0.0049.
Values may be sent and summed in bfloat16 or wider, within the bound.
A program may use at most 128 MiB of HBM per device.

v0:
```python
import jax
import jax.numpy as jnp
from jax import lax
from jax.sharding import PartitionSpec as P

KVL = 512
FF = 2048


softmax_scale = 0.1353


def attend(queries, key_rows, lengths):
    scores = (
        jnp.einsum("rshc,rtc->rsht", queries, key_rows, preferred_element_type=jnp.float32)
        * softmax_scale
    )
    in_range = jnp.arange(key_rows.shape[1])[None, :] < lengths[:, None]
    scores = jnp.where(in_range[:, None, None, :], scores, -1e30)
    row_max = jnp.max(scores, axis=-1, keepdims=True)
    raised = jnp.exp(scores - row_max)
    probabilities = (raised / jnp.sum(raised, axis=-1, keepdims=True)).astype(jnp.bfloat16)
    return jnp.einsum(
        "rsht,rtc->rshc", probabilities, key_rows[..., :KVL], preferred_element_type=jnp.float32
    ).astype(jnp.bfloat16)


def expert_rows(rows_in, w_gate, w_up, w_down):
    gate_act = jnp.dot(rows_in, w_gate[0], preferred_element_type=jnp.float32)
    up_act = jnp.dot(rows_in, w_up[0], preferred_element_type=jnp.float32)
    activation = (jax.nn.silu(gate_act) * up_act).astype(jnp.bfloat16)
    return jnp.dot(activation, w_down[0], preferred_element_type=jnp.float32)


def local(
    queries,
    cache_pool,
    mig_block,
    block_table,
    lengths,
    hidden_states,
    routes,
    route_weight,
    w_gate,
    w_up,
    w_down,
):
    own_blocks = cache_pool.shape[0]
    targets = mig_block[0]
    outgoing = jnp.where(
        (targets < own_blocks)[:, None, None],
        cache_pool[jnp.minimum(targets, own_blocks - 1)],
        jnp.zeros((), jnp.bfloat16),
    )
    arrived = lax.all_to_all(outgoing, "ep", split_axis=0, concat_axis=0, tiled=True)
    working = jnp.concatenate([cache_pool, arrived], axis=0)
    key_rows = working[block_table].reshape(block_table.shape[0], -1, cache_pool.shape[2])
    attn_out = attend(queries, key_rows, lengths)
    token_count, model_width = hidden_states.shape
    top_count = routes.shape[1]
    span_count = FF // w_gate.shape[2]
    devices = lax.axis_size("ep")
    experts = devices // span_count
    capacity = token_count * top_count // experts
    matches = routes[:, :, None] == jnp.arange(experts, dtype=jnp.int32)[None, None, :]
    gate_table = jnp.sum(
        jnp.where(matches, route_weight[:, :, None], jnp.zeros((), jnp.bfloat16)), axis=1
    )
    all_hidden, all_gates = (
        lax.all_gather(hidden_states, "ep", axis=0, tiled=True),
        lax.all_gather(gate_table, "ep", axis=0, tiled=True),
    )
    own_expert = lax.axis_index("ep") // span_count
    column = lax.dynamic_index_in_dim(all_gates, own_expert, 1, keepdims=False)
    selected = column != 0
    rank_ids = jnp.cumsum(selected.astype(jnp.int32)) - 1
    slot_total = devices * capacity
    slot_ids = (
        jnp.zeros((slot_total,), jnp.int32)
        .at[jnp.where(selected, rank_ids, slot_total)]
        .set(jnp.arange(column.shape[0], dtype=jnp.int32), mode="drop")
    )
    expert_out = expert_rows(all_hidden[slot_ids], w_gate, w_up, w_down)
    scaled = column[slot_ids].astype(jnp.float32)[:, None] * expert_out
    partial_term = jnp.zeros((column.shape[0], model_width), jnp.float32).at[slot_ids].add(scaled)
    moe_out = lax.psum_scatter(partial_term, "ep", scatter_dimension=0, tiled=True)
    return (attn_out, moe_out.astype(jnp.bfloat16))


def solution(mesh):
    placed = (
        P(("group", "ep"), None, None, None),
        P(("group", "ep"), None, None),
        P(("group", "ep"), None),
        P(("group", "ep"), None),
        P(("group", "ep")),
        P(("group", "ep"), None),
        P(("group", "ep"), None),
        P(("group", "ep"), None),
        P("ep", None, None),
        P("ep", None, None),
        P("ep", None, None),
    )
    return jax.shard_map(
        local,
        mesh=mesh,
        in_specs=placed,
        out_specs=(P(("group", "ep"), None, None, None), P(("group", "ep"), None)),
        check_vma=False,
    )
```

profile of v0, /device:TPU:0, one launch (start us, length us, event | category | flops | bytes accessed | tf_op | source)
XLA Modules:
  0.0 238.7 jit_solution(5441678767183783392)
XLA Ops:
  7.2 0.0 copy-start
  7.2 0.0 all-gather.3.cloned.1.call-start
  7.2 0.7 all-gather.3.cloned.1.call-update
  7.9 0.0 reduce-scatter.2.cloned.1.call-start
  8.0 0.7 fusion.36
  8.7 43.3 %all-gather = bf16[32,8,4]{1,2,0:T(4,128)(2,1)S(1)} all-gather(bf16[1,8,4]{1,2,0:T(4,128)(2,1)S(1)} %bitcast.58), channel_id=1, replica_groups=mesh['group'=1,'ep'=32] {'ep'}, dimensions={0}, use_global_device_ids=true | all-gather | bytes 2112 | tf_op jit(solution)/shard_map/all_gather | solution.py:71
  52.0 0.1 reshape.157
  52.1 0.3 reduce-window.9
  52.4 0.1 slice.11
  52.5 0.1 slice_reduce_fusion
  52.6 0.1 add_add_fusion
  52.7 1.4 scatter_custom_fusion
  54.2 1.2 gather_fusion.2
  55.4 13.9 %all-gather.3.cloned.1.call-done = bf16[256,3584]{1,0:T(8,128)(2,1)} async-done(((bf16[8,3584]{1,0:T(8,128)(2,1)}), bf16[256,3584]{1,0:T(8,128)(2,1)}) %all-gather.3.cloned.1.call-update) | async-done | bytes 1835024 | tf_op jit(solution)/shard_map/all_gather | solution.py:70
  69.4 3.8 %gather_fusion.3 = bf16[128,3584]{1,0:T(8,128)(2,1)S(1)} fusion(bf16[256,3584]{1,0:T(8,128)(2,1)} %all-gather.3.cloned.1.call-done, s32[1024]{0:T(1024)S(1)} %pad_clamp_fusion), kind=kCustom, calls=%fused_computation.3 | custom fusion | bytes 1835520 | tf_op jit(solution)/shard_map/gather | solution.py:83
  73.2 1.9 fusion.12
  75.1 0.0 copy-done
  75.1 3.9 %convolution_multiply_fusion = f32[128,3584]{1,0:T(8,128)} fusion(bf16[1,256,3584]{2,1,0:T(8,128)(2,1)S(1)} %copy-done, bf16[128,3584]{1,0:T(8,128)(2,1)S(1)} %gather_fusion.3, bf16[1,3584,256]{2,1,0:T(8,128)(2,1)} %param.20, f32[128]{0:T(128)S(1)} %convert_element_type.32, f32[128,256]{1,0:T(8,128)S(1)} %fusion.12), kind=kOutput, calls=%fused_computation.9 | convolution fusion | flops 470417408 | bytes 6554112 | tf_op jit(solution)/shard_map/dot_general | solution.py:32
  79.0 0.0 copy-start.5
  79.0 5.9 %scatter_custom_fusion.1 = f32[256,3584]{1,0:T(8,128)} fusion(s32[128]{0:T(128)S(1)} %compare_select_fusion.2, f32[128,3584]{1,0:T(8,128)} %convolution_multiply_fusion, f32[]{:T(128)} %constant.26.clone.1), kind=kCustom, calls=%fused_computation.25 | custom fusion | flops 458752 | bytes 3670528 | tf_op jit(solution)/shard_map/scatter-add | solution.py:85
  84.9 0.0 reduce-scatter.2.cloned.1.call-update
  84.9 0.0 copy-done.5
  85.0 5.0 %gather_fusion = bf16[32,64,576]{2,1,0:T(8,128)(2,1)} fusion(bf16[68,64,576]{2,1,0:T(8,128)(2,1)} %param.12, s32[1024]{0:T(1024)S(1)} %pad_clamp_fusion.2), kind=kCustom, calls=%fused_computation | custom fusion | bytes 4718720 | tf_op jit(solution)/shard_map/gather | solution.py:52
  90.0 3.6 %broadcast_select_fusion = bf16[32,64,576]{2,1,0:T(8,128)(2,1)} fusion(bf16[32,64,576]{2,1,0:T(8,128)(2,1)} %gather_fusion, pred[32]{0:T(512)(128)(4,1)S(1)} %compare_bitcast_fusion), kind=kLoop, calls=%fused_computation.18 | loop fusion | flops 1179648 | bytes 4718624 | tf_op jit(solution)/shard_map/jit(_where)/select_n | solution.py:50
  93.6 0.0 copy-start.2
  93.6 0.0 copy-start.3
  93.6 3.9 %all-to-all-start = ((bf16[32,64,576]{2,1,0:T(8,128)(2,1)}), bf16[32,64,576]{2,1,0:T(8,128)(2,1)}, u32[]{:S(2)}, u32[]{:S(2)}) async-start(bf16[32,64,576]{2,1,0:T(8,128)(2,1)} %broadcast_select_fusion), calls=%async_computation | async-start | bytes 5242880 | tf_op jit(solution)/shard_map/all_to_all | solution.py:55
  97.5 0.0 copy-done.2
  97.5 0.1 reshape.112
  97.6 0.0 copy-done.3
  97.6 0.1 iota_compare_fusion
  97.7 67.0 %all-to-all-done = bf16[32,64,576]{2,1,0:T(8,128)(2,1)} async-done(((bf16[32,64,576]{2,1,0:T(8,128)(2,1)}), bf16[32,64,576]{2,1,0:T(8,128)(2,1)}, u32[]{:S(2)}, u32[]{:S(2)}) %all-to-all-start) | async-done | bytes 2359328 | tf_op jit(solution)/shard_map/all_to_all | solution.py:55
  164.7 7.7 %pad_maximum_fusion = bf16[100,64,576]{2,1,0:T(8,128)(2,1)} fusion(bf16[32,64,576]{2,1,0:T(8,128)(2,1)} %all-to-all-done, bf16[68,64,576]{2,1,0:T(8,128)(2,1)} %param.12), kind=kLoop, calls=%fused_computation.7 | loop fusion | flops 3686400 | bytes 14745600 | tf_op jit(solution)/shard_map/concatenate | solution.py:56
  172.3 0.0 copy-start.4
  172.3 9.8 %gather_fusion.1 = bf16[68,64,576]{2,1,0:T(8,128)(2,1)} fusion(bf16[100,64,576]{2,1,0:T(8,128)(2,1)} %pad_maximum_fusion, s32[1024]{0:T(1024)S(1)} %pad_clamp_fusion.1), kind=kCustom, calls=%fused_computation.1 | custom fusion | bytes 10027280 | tf_op jit(solution)/shard_map/gather | solution.py:57
  182.1 0.0 copy-done.4
  182.1 4.7 %fusion.2 = f32[4,1088,2,128]{3,1,2,0:T(8,128)S(1)} fusion(bf16[4,1088,576,1]{2,1,3,0:T(8,128)(2,1)} %bitcast.55, bf16[4,2,128,576]{2,3,1,0:T(8,128)(2,1)S(1)} %copy-done.4, pred[4,1088]{1,0:T(4,128)(4,1)S(1)} %iota_compare_fusion), kind=kOutput, calls=%fused_computation.11 | convolution fusion | flops 1285685248 | bytes 10653952 | tf_op jit(solution)/shard_map/rshc,rtc->rsht/dot_general | solution.py:15
  186.8 0.0 copy-start.1
  186.8 2.0 copy-done.1
  188.8 0.9 fusion.43
  189.7 6.3 %fusion.16 = bf16[4,2,128,512]{3,2,1,0:T(8,128)(2,1)} fusion(bf16[4,1088,576]{2,1,0:T(8,128)(2,1)} %bitcast.56, f32[4,2,128]{2,1,0:T(2,128)S(1)} %fusion.43, f32[4,1088,2,128]{3,1,2,0:T(8,128)} %copy-done.1), kind=kOutput, calls=%fused_computation.27 | convolution fusion | flops 1144719360 | bytes 9965568 | tf_op jit(solution)/shard_map/rsht,rtc->rshc/dot_general | solution.py:23
  196.1 34.2 %reduce-scatter.2.cloned.1.call-done = f32[8,3584]{1,0:T(8,128)} async-done(((f32[256,3584]{1,0:T(8,128)}), f32[8,3584]{1,0:T(8,128)}) %reduce-scatter.2.cloned.1.call-update) | async-done | bytes 114704 | tf_op jit(solution)/shard_map/reduce_scatter | solution.py:86
  230.3 1.5 convert_element_type.34
  (14 shorter events, 0.1 us)
Async XLA Ops:
  7.2 67.9 %copy-start = (bf16[1,256,3584]{2,1,0:T(8,128)(2,1)S(1)}, bf16[1,256,3584]{2,1,0:T(8,128)(2,1)}, u32[]{:S(2)}) copy-start(bf16[1,256,3584]{2,1,0:T(8,128)(2,1)} %param.21) | copy-start | bytes 5505028
  7.2 62.2 %all-gather.3.cloned.1.call-start = ((), (), s32[]{:S(2)}) async-start(), calls=%async_computation.2 | async-start | bytes 1892352 | tf_op jit(solution)/shard_map/all_gather | solution.py:70
  7.9 222.4 %reduce-scatter.2.cloned.1.call-start = ((), (), s32[]{:S(2)}) async-start(), calls=%async_computation.3 | async-start | bytes 3784704 | tf_op jit(solution)/shard_map/reduce_scatter | solution.py:86
  79.0 5.9 %copy-start.5 = (s32[1,32]{1,0:T(1,128)S(1)}, s32[1,32]{1,0:T(1,128)}, u32[]{:S(2)}) copy-start(s32[1,32]{1,0:T(1,128)} %param.13) | copy-start | bytes 388
  93.6 3.9 %copy-start.2 = (s32[4,17]{1,0:T(4,128)S(1)}, s32[4,17]{1,0:T(4,128)}, u32[]{:S(2)}) copy-start(s32[4,17]{1,0:T(4,128)} %param.14) | copy-start | bytes 820
  93.6 4.0 %copy-start.3 = (s32[4]{0:T(128)S(1)}, s32[4]{0:T(128)}, u32[]{:S(2)}) copy-start(s32[4]{0:T(128)} %param.15) | copy-start | bytes 52
  93.6 71.0 %all-to-all-start = ((bf16[32,64,576]{2,1,0:T(8,128)(2,1)}), bf16[32,64,576]{2,1,0:T(8,128)(2,1)}, u32[]{:S(2)}, u32[]{:S(2)}) async-start(bf16[32,64,576]{2,1,0:T(8,128)(2,1)} %broadcast_select_fusion), calls=%async_computation | async-start | bytes 5242880 | tf_op jit(solution)/shard_map/all_to_all | solution.py:55
  172.3 9.8 %copy-start.4 = (bf16[4,2,128,576]{2,3,1,0:T(8,128)(2,1)S(1)}, bf16[4,2,128,576]{2,3,1,0:T(8,128)(2,1)}, u32[]{:S(2)}) copy-start(bf16[4,2,128,576]{2,3,1,0:T(8,128)(2,1)} %param.11) | copy-start | bytes 3538948
  186.8 2.0 copy-start.1
Sparse Core Ops, SparseCore 0:
  10.8 58.5 all-gather.2
  85.0 145.1 reduce-scatter.1
where the time goes:
time: 239 us
  waiting for transfers between devices  116 us (49%)
  blocking collectives  43.3 us (18%)
  local copies, waits for them, and re-layouts  23.7 us (10%)
  other arithmetic  20.8 us (9%)
  matrix products  16.8 us (7%)
  between operations  14.2 us (6%)
  starting transfers between devices  3.93 us (2%)
    all_to_all x1, waiting for transfers between devices, local(): lax.all_to_all(outgoing, 'ep', split_axis=0, concat_axis=0, tiled=True)  67 us
    all_gather x1, blocking collectives, local(): lax.all_gather(gate_table, 'ep', axis=0, tiled=True)  43.3 us
    reduce_scatter x1, waiting for transfers between devices, local(): lax.psum_scatter(partial_term, 'ep', scatter_dimension=0, tiled=True)  34.2 us
    all_gather x1, waiting for transfers between devices, local(): lax.all_gather(hidden_states, 'ep', axis=0, tiled=True)  13.9 us
    gather x1, local copies, waits for them, and re-layouts, local(): working[block_table].reshape(block_table.shape[0], -1, cache_pool.shape[2])  9.8 us
    concatenate x1, other arithmetic, local(): working = jnp.concatenate([cache_pool, arrived], axis=0)  7.65 us
    dot_general x1, matrix products, attend(): jnp.einsum('rsht,rtc->rshc', probabilities, key_rows[..., :KVL], preferre...  6.34 us
    scatter-add x1, other arithmetic, local(): jnp.zeros((column.shape[0], model_width), jnp.float32).at[slot_ids]  5.87 us
  transfers between devices with their start and end apart: 3, of which 3 were waited for; matrix products, arithmetic and copies ran while one was open for 18% of the time, Pallas kernels for 0%

commit v1 on v0

v1 whole, which is shorter than its diff:
```python
import functools
import math

import jax
import jax.numpy as jnp
from jax import lax
from jax.experimental import pallas as pl
from jax.experimental.pallas import tpu as pltpu
from jax.sharding import PartitionSpec as P

KVL = 512
FF = 2048
SLOT = 4
QUARTERS = 4
LANES = 128
MESH = pl.DeviceIdType.MESH

softmax_scale = 0.1353


def send(src, dst, send_sem, recv_sem, target):
    return pltpu.make_async_remote_copy(
        src_ref=src,
        dst_ref=dst,
        send_sem=send_sem,
        recv_sem=recv_sem,
        device_id={"ep": target},
        device_id_type=MESH,
    )


def spread(quarter, rows, cols, transposed):
    shape = (cols, rows) if transposed else (rows, cols)
    flat = lax.broadcasted_iota(jnp.int32, shape, 1 if transposed else 0)
    wide = lax.broadcasted_iota(jnp.int32, shape, 0 if transposed else 1)
    match = flat + (flat >> 2) * 12 + quarter * SLOT == wide
    return jnp.where(match, 1.0, 0.0).astype(jnp.bfloat16)


def exchange_kernel(
    n,
    split,
    mig_ref,
    pool_ref,
    hidden_ref,
    pick_ref,
    combine_ref,
    gate_ref,
    up_ref,
    down_ref,
    arrived_ref,
    moe_ref,
    pool_v,
    outgoing,
    gate_v,
    up_v,
    down_v,
    token_out,
    token_in,
    gathered,
    part_out,
    part_in,
    back_out,
    back_in,
    load_sem,
    mig_send,
    mig_recv,
    token_send,
    token_recv,
    gather_send,
    gather_recv,
    part_send,
    part_recv,
    back_send,
    back_recv,
):
    me = lax.axis_index("ep")
    planes = n // split
    plane, place = me // split, me % split
    own_blocks = pool_ref.shape[0]
    width = hidden_ref.shape[1] // QUARTERS
    chunk = planes * SLOT
    wide = planes * SLOT * QUARTERS

    loads = [
        pltpu.make_async_copy(pool_ref, pool_v, load_sem.at[0]),
        pltpu.make_async_copy(gate_ref, gate_v, load_sem.at[1]),
        pltpu.make_async_copy(up_ref, up_v, load_sem.at[2]),
        pltpu.make_async_copy(down_ref, down_v, load_sem.at[3]),
    ]
    for load in loads:
        load.start()

    barrier = pltpu.get_barrier_semaphore()

    def greet(k, carry):
        pl.semaphore_signal(
            barrier, inc=1, device_id={"ep": (me + k) % n}, device_id_type=MESH
        )
        return carry

    lax.fori_loop(1, n, greet, 0)

    messages = jnp.zeros((wide, width), jnp.float32)
    for q in range(QUARTERS):
        messages += jnp.dot(
            pick_ref[q],
            hidden_ref[:, q * width : (q + 1) * width],
            preferred_element_type=jnp.float32,
        )
    token_out[...] = messages.astype(jnp.bfloat16).reshape(token_out.shape)
    token_in[plane] = token_out[plane]

    pl.semaphore_wait(barrier, n - 1)

    def token_copy(k):
        other = (plane + k) % planes
        return send(
            token_out.at[other],
            token_in.at[plane],
            token_send.at[k],
            token_recv.at[plane],
            other * split + place,
        )

    for k in range(1, planes):
        token_copy(k).start()

    loads[0].wait()

    def mig_copy(k):
        target = (me + k) % n
        return send(
            outgoing.at[k], arrived_ref.at[me], mig_send.at[k], mig_recv.at[me], target
        )

    def mig_start(k, carry):
        target = (me + k) % n
        block = jnp.minimum(mig_ref[0, target], own_blocks - 1)
        for c in range(KVL // LANES):
            outgoing[k, c * 64 : (c + 1) * 64, :] = pool_v[
                block, :, c * LANES : (c + 1) * LANES
            ]
        tail = pool_v[block, :, KVL:]
        outgoing[k, 256:288, :] = jnp.concatenate([tail[:32], tail[32:]], axis=1)
        mig_copy(k).start()
        return carry

    far = n - split
    lax.fori_loop(split, split + far // 2, mig_start, 0)

    for k in range(1, planes):
        other = (plane + k) % planes
        send(
            token_out.at[k], token_in.at[other], token_send.at[k], token_recv.at[other], me
        ).wait_recv()
    arrived_tokens = token_in[...].reshape(wide, width)
    for q in range(QUARTERS):
        gathered[place, :, q * width : (q + 1) * width] = jnp.dot(
            spread(q, chunk, wide, False),
            arrived_tokens,
            preferred_element_type=jnp.float32,
        ).astype(jnp.bfloat16)

    def gather_copy(k):
        other = (place + k) % split
        return send(
            gathered.at[place],
            gathered.at[place],
            gather_send.at[k],
            gather_recv.at[place],
            plane * split + other,
        )

    for k in range(1, split):
        gather_copy(k).start()

    lax.fori_loop(split + far // 2, n, mig_start, 0)

    for load in loads[1:]:
        load.wait()
    for k in range(1, split):
        other = (place + k) % split
        send(
            gathered.at[place],
            gathered.at[other],
            gather_send.at[k],
            gather_recv.at[other],
            me,
        ).wait_recv()

    rows = gathered[...].reshape(split * chunk, gathered.shape[2])
    gate_act = jnp.dot(rows, gate_v[0], preferred_element_type=jnp.float32)
    up_act = jnp.dot(rows, up_v[0], preferred_element_type=jnp.float32)
    activation = (gate_act / (1.0 + jnp.exp(-gate_act)) * up_act).astype(jnp.bfloat16)
    for q in range(QUARTERS):
        columns = slice(q * width, (q + 1) * width)
        part_out[:, :, columns] = (
            jnp.dot(activation, down_v[0, :, columns], preferred_element_type=jnp.float32)
            .astype(jnp.bfloat16)
            .reshape(split, chunk, width)
        )

    def part_copy(k):
        other = (place + k) % split
        return send(
            part_out.at[other],
            part_in.at[place],
            part_send.at[k],
            part_recv.at[place],
            plane * split + other,
        )

    for k in range(1, split):
        part_copy(k).start()
    part_in[place] = part_out[place]

    lax.fori_loop(1, split, mig_start, 0)

    for k in range(1, split):
        other = (place + k) % split
        send(
            part_out.at[other], part_in.at[other], part_send.at[k], part_recv.at[other], me
        ).wait_recv()
    messages = jnp.zeros((wide, width), jnp.float32)
    for q in range(QUARTERS):
        columns = slice(q * width, (q + 1) * width)
        total = part_in[0, :, columns].astype(jnp.float32)
        for p in range(1, split):
            total += part_in[p, :, columns].astype(jnp.float32)
        messages += jnp.dot(
            spread(q, chunk, wide, True),
            total.astype(jnp.bfloat16),
            preferred_element_type=jnp.float32,
        )
    back_out[...] = messages.astype(jnp.bfloat16).reshape(back_out.shape)
    back_in[plane] = back_out[plane]

    def back_copy(k):
        other = (plane + k) % planes
        return send(
            back_out.at[other],
            back_in.at[plane],
            back_send.at[k],
            back_recv.at[plane],
            other * split + place,
        )

    for k in range(1, planes):
        back_copy(k).start()
    for k in range(1, planes):
        other = (plane + k) % planes
        send(
            back_out.at[k], back_in.at[other], back_send.at[k], back_recv.at[other], me
        ).wait_recv()
    returned = back_in[...].reshape(wide, width)
    for q in range(QUARTERS):
        moe_ref[:, q * width : (q + 1) * width] = jnp.dot(
            combine_ref[q], returned, preferred_element_type=jnp.float32
        ).astype(jnp.bfloat16)

    for k in range(1, planes):
        token_copy(k).wait_send()
        back_copy(k).wait_send()
    for k in range(1, split):
        gather_copy(k).wait_send()
        part_copy(k).wait_send()

    def mig_wait(k, carry):
        source = (me + k) % n
        send(
            outgoing.at[k], arrived_ref.at[source], mig_send.at[k], mig_recv.at[source], me
        ).wait_recv()
        mig_copy(k).wait_send()
        return carry

    lax.fori_loop(1, n, mig_wait, 0)


def exchange(cache_pool, mig_block, hidden_states, pick, combine, w_gate, w_up, w_down, n, split):
    blocks, positions, entries = cache_pool.shape
    tokens, model_width = hidden_states.shape
    packed = positions * entries // LANES
    planes = n // split
    chunk = planes * SLOT
    width = model_width // QUARTERS
    any_space = pl.BlockSpec(memory_space=pl.ANY)
    vmem = pl.BlockSpec(memory_space=pltpu.VMEM)
    bf16 = jnp.bfloat16
    dma = pltpu.SemaphoreType.DMA
    return pl.pallas_call(
        functools.partial(exchange_kernel, n, split),
        out_shape=(
            jax.ShapeDtypeStruct((n, packed, LANES), bf16),
            jax.ShapeDtypeStruct((tokens, model_width), bf16),
        ),
        in_specs=[
            pl.BlockSpec(memory_space=pltpu.SMEM),
            any_space,
            vmem,
            vmem,
            vmem,
            any_space,
            any_space,
            any_space,
        ],
        out_specs=(any_space, vmem),
        scratch_shapes=[
            pltpu.VMEM(cache_pool.shape, bf16),
            pltpu.VMEM((n, packed, LANES), bf16),
            pltpu.VMEM(w_gate.shape, bf16),
            pltpu.VMEM(w_up.shape, bf16),
            pltpu.VMEM(w_down.shape, bf16),
            pltpu.VMEM((planes, SLOT * QUARTERS, width), bf16),
            pltpu.VMEM((planes, SLOT * QUARTERS, width), bf16),
            pltpu.VMEM((split, chunk, model_width), bf16),
            pltpu.VMEM((split, chunk, model_width), bf16),
            pltpu.VMEM((split, chunk, model_width), bf16),
            pltpu.VMEM((planes, SLOT * QUARTERS, width), bf16),
            pltpu.VMEM((planes, SLOT * QUARTERS, width), bf16),
            dma((4,)),
            dma((n,)),
            dma((n,)),
            dma((planes,)),
            dma((planes,)),
            dma((split,)),
            dma((split,)),
            dma((split,)),
            dma((split,)),
            dma((planes,)),
            dma((planes,)),
        ],
        compiler_params=pltpu.CompilerParams(
            collective_id=0, has_side_effects=True, vmem_limit_bytes=48 * 1024 * 1024
        ),
        name="exchange",
    )(mig_block, cache_pool, hidden_states, pick, combine, w_gate, w_up, w_down)


def attend_kernel(sizes, table_ref, lengths_ref, queries_ref, pool_ref, arrived_ref, out_ref, keys):
    request = pl.program_id(0)
    own_blocks, positions, entries = pool_ref.shape
    length = lengths_ref[request]
    used = (length + positions - 1) // positions

    @pl.when(request == 0)
    def _():
        keys[...] = jnp.zeros_like(keys)

    def place_block(b, carry):
        entry = table_ref[request, b]
        start = pl.multiple_of(b * positions, positions)

        @pl.when(entry < own_blocks)
        def _():
            keys[pl.ds(start, positions), :] = pool_ref[entry]

        @pl.when(entry >= own_blocks)
        def _():
            source = entry - own_blocks
            for c in range(KVL // LANES):
                keys[pl.ds(start, positions), c * LANES : (c + 1) * LANES] = arrived_ref[
                    source, c * positions : (c + 1) * positions, :
                ]
            tail = arrived_ref[source, 256:288, :]
            keys[pl.ds(start, 32), KVL:] = tail[:, :64]
            keys[pl.ds(start + 32, 32), KVL:] = tail[:, 64:]

        return carry

    lax.fori_loop(0, used, place_block, 0)
    steps, heads = queries_ref.shape[1], queries_ref.shape[2]
    queries = queries_ref[0].reshape(steps * heads, entries)

    def attend(count):
        rows = count * positions
        scores = lax.dot_general(
            queries,
            keys[:rows, :],
            (((1,), (1,)), ((), ())),
            preferred_element_type=jnp.float32,
        ) * (softmax_scale * math.log2(math.e))
        where = lax.broadcasted_iota(jnp.int32, scores.shape, 1)
        scores = jnp.where(where < length, scores, -1e30)
        raised = jnp.exp2(scores - jnp.max(scores, axis=1, keepdims=True))
        total = jnp.sum(raised, axis=1, keepdims=True)
        out = jnp.dot(
            raised.astype(jnp.bfloat16), keys[:rows, :KVL], preferred_element_type=jnp.float32
        )
        out_ref[0] = (out / total).astype(jnp.bfloat16).reshape(steps, heads, KVL)

    low = 0
    for count in sizes:

        @pl.when((used > low) & (used <= count))
        def _():
            attend(count)

        low = count


def attention(queries, cache_pool, arrived, block_table, lengths):
    requests, steps, heads, entries = queries.shape
    blocks = block_table.shape[1]
    sizes = tuple(c for c in (4, 8, 12) if c < blocks) + (blocks,)
    smem = pl.BlockSpec(memory_space=pltpu.SMEM)
    vmem = pl.BlockSpec(memory_space=pltpu.VMEM)
    return pl.pallas_call(
        functools.partial(attend_kernel, sizes),
        grid=(requests,),
        out_shape=jax.ShapeDtypeStruct((requests, steps, heads, KVL), jnp.bfloat16),
        in_specs=[
            smem,
            smem,
            pl.BlockSpec((1, steps, heads, entries), lambda r: (r, 0, 0, 0)),
            vmem,
            vmem,
        ],
        out_specs=pl.BlockSpec((1, steps, heads, KVL), lambda r: (r, 0, 0, 0)),
        scratch_shapes=[pltpu.VMEM((blocks * cache_pool.shape[1], entries), jnp.bfloat16)],
        compiler_params=pltpu.CompilerParams(vmem_limit_bytes=48 * 1024 * 1024),
        name="attention",
    )(block_table, lengths, queries, cache_pool, arrived)


def local(
    queries,
    cache_pool,
    mig_block,
    block_table,
    lengths,
    hidden_states,
    routes,
    route_weight,
    w_gate,
    w_up,
    w_down,
):
    n = lax.axis_size("ep")
    split = FF // w_gate.shape[2]
    experts = n // split
    tokens = hidden_states.shape[0]
    ids = jnp.arange(experts, dtype=jnp.int32)
    matches = routes[:, :, None] == ids[None, None, :]
    hit = jnp.any(matches, axis=1)
    weight = jnp.sum(jnp.where(matches, route_weight[:, :, None], jnp.zeros((), jnp.bfloat16)), axis=1)
    order = jnp.arange(tokens)
    earlier = order[None, :] < order[:, None]
    rank = jnp.sum((earlier[:, :, None] & hit[None, :, :]).astype(jnp.int32), axis=1)
    slots = jnp.arange(SLOT)
    chosen = hit[:, :, None] & (rank[:, :, None] == slots)
    quarters = jnp.arange(QUARTERS)
    same = quarters[:, None] == quarters[None, :]
    wide = experts * QUARTERS * SLOT
    both = same[:, None, None, :, None] & chosen[None, :, :, None, :]
    combine = jnp.where(
        both, weight[None, :, :, None, None], jnp.zeros((), jnp.bfloat16)
    ).reshape(QUARTERS, tokens, wide)
    pick = both.astype(jnp.bfloat16).reshape(QUARTERS, tokens, wide).swapaxes(1, 2)
    arrived, moe_out = exchange(
        cache_pool, mig_block, hidden_states, pick, combine, w_gate, w_up, w_down, n, split
    )
    attn_out = attention(queries, cache_pool, arrived, block_table, lengths)
    return attn_out, moe_out


def solution(mesh):
    placed = (
        P(("group", "ep"), None, None, None),
        P(("group", "ep"), None, None),
        P(("group", "ep"), None),
        P(("group", "ep"), None),
        P(("group", "ep")),
        P(("group", "ep"), None),
        P(("group", "ep"), None),
        P(("group", "ep"), None),
        P("ep", None, None),
        P("ep", None, None),
        P("ep", None, None),
    )
    return jax.shard_map(
        local,
        mesh=mesh,
        in_specs=placed,
        out_specs=(P(("group", "ep"), None, None, None), P(("group", "ep"), None)),
        check_vma=False,
    )
```

time: 239 us -> 97.6 us (0.41)
  the two profiles are of different devices: /device:TPU:0 before, /device:TPU:5 now
where the time goes in v1:
time: 97.6 us; the launch traced here: 97.9 us
  Pallas kernels  88 us (90%)
  local copies, waits for them, and re-layouts  7.32 us (8%)
  other arithmetic  1.81 us (2%)
    pallas_call x1, Pallas kernels, exchange(): pl.pallas_call(functools.partial(exchange_kernel, n, split), out_shape=(j...  78.2 us
    pallas_call x1, Pallas kernels, attention(): pl.pallas_call(functools.partial(attend_kernel, sizes), grid=(requests,),...  9.87 us
    unnamed x18, local copies, waits for them, and re-layouts  6.98 us

profile of v1, /device:TPU:5, one launch (start us, length us, event | category | flops | bytes accessed | tf_op | source)
XLA Modules:
  0.0 97.9 jit_solution(4429727198782588102)
XLA Ops:
  0.6 0.0 copy-start.1
  0.6 0.0 copy-start.4
  0.7 0.0 copy-start.6
  0.7 0.8 fusion.2
  1.5 0.7 fusion.3
  2.2 0.2 convert_reduce_fusion
  2.4 0.1 copy.23
  2.4 0.1 and.61
  2.5 0.1 and.62
  2.7 0.1 copy.24
  2.7 0.1 and_convert_fusion.pick_ref
  2.9 1.7 %copy.25.queries_ref = bf16[4,2,128,576]{3,2,1,0:T(8,128)(2,1)S(1)} copy(bf16[4,2,128,576]{2,3,1,0:T(8,128)(2,1)} %param.11) | data formatting | bytes 2359296 | tf_op args[0]
  4.5 0.0 copy-done.1
  4.6 0.0 copy-done.4
  4.6 0.0 copy-done.6
  4.6 0.0 copy-start.2
  4.6 1.5 %copy-done.2 = bf16[1,3584,256]{2,1,0:T(8,128)(2,1)S(1)} copy-done((bf16[1,3584,256]{2,1,0:T(8,128)(2,1)S(1)}, bf16[1,3584,256]{2,1,0:T(8,128)(2,1)}, u32[]{:S(2)}) %copy-start.2) | copy-done | bytes 1835032
  6.1 0.0 copy-start.3
  6.1 1.5 %copy-done.3 = bf16[1,256,3584]{2,1,0:T(8,128)(2,1)S(1)} copy-done((bf16[1,256,3584]{2,1,0:T(8,128)(2,1)S(1)}, bf16[1,256,3584]{2,1,0:T(8,128)(2,1)}, u32[]{:S(2)}) %copy-start.3) | copy-done | bytes 1835032
  7.6 0.0 copy-start.5
  7.6 0.0 copy-start.7
  7.6 78.2 %exchange.1 = (bf16[32,288,128]{2,1,0:T(8,128)(2,1)}, bf16[8,3584]{1,0:T(8,128)(2,1)S(1)}) custom-call(s32[1,32]{1,0:T(1,128)S(1)} %copy-done.6, bf16[68,64,576]{2,1,0:T(8,128)(2,1)} %pool_ref.3, bf16[8,3584]{1,0:T(8,128)(2,1)S(1)} %copy-done.4, bf16[4,64,8]{2,1,0:T(8,128)(2,1)S(1)} %and_convert_fusion.pick_ref, ...), custom_call_target="tpu_custom_call" | custom-call | tf_op jit(solution)/shard_map/exchange/pallas_call | solution.py:291
  85.8 0.0 copy-done.5
  85.8 0.0 copy-done.7
  85.8 0.0 copy-start
  85.8 1.7 %copy-done = bf16[32,288,128]{2,1,0:T(8,128)(2,1)S(1)} copy-done((bf16[32,288,128]{2,1,0:T(8,128)(2,1)S(1)}, bf16[32,288,128]{2,1,0:T(8,128)(2,1)}, u32[]{:S(2)}) %copy-start) | copy-done | bytes 2359320
  87.4 9.9 %attention.1 = bf16[4,2,128,512]{3,2,1,0:T(8,128)(2,1)} custom-call(s32[4,17]{1,0:T(4,128)S(1)} %copy-done.5, s32[4]{0:T(128)S(1)} %copy-done.7, bf16[4,2,128,576]{3,2,1,0:T(8,128)(2,1)S(1)} %copy.25.queries_ref, bf16[68,64,576]{2,1,0:T(8,128)(2,1)} %pool_ref.3, bf16[32,288,128]{2,1,0:T(8,128)(2,1)S(1)} %copy-done), custom_call_target="tpu_custom_call" | custom-call | tf_op jit(solution)/shard_map/attention/pallas_call | solution.py:408
  97.3 0.6 copy.27
  (6 shorter events, 0.0 us)
Async XLA Ops:
  0.6 3.9 %copy-start.1 = (bf16[1,3584,256]{2,1,0:T(8,128)(2,1)S(1)}, bf16[1,3584,256]{2,1,0:T(8,128)(2,1)}, u32[]{:S(2)}) copy-start(bf16[1,3584,256]{2,1,0:T(8,128)(2,1)} %gate_ref.1) | copy-start | bytes 5505028
  0.6 3.9 %copy-start.4 = (bf16[8,3584]{1,0:T(8,128)(2,1)S(1)}, bf16[8,3584]{1,0:T(8,128)(2,1)}, u32[]{:S(2)}) copy-start(bf16[8,3584]{1,0:T(8,128)(2,1)} %hidden_ref.1) | copy-start | bytes 172036
  0.7 3.9 %copy-start.6 = (s32[1,32]{1,0:T(1,128)S(1)}, s32[1,32]{1,0:T(1,128)}, u32[]{:S(2)}) copy-start(s32[1,32]{1,0:T(1,128)} %mig_ref.1) | copy-start | bytes 388
  4.6 1.5 %copy-start.2 = (bf16[1,3584,256]{2,1,0:T(8,128)(2,1)S(1)}, bf16[1,3584,256]{2,1,0:T(8,128)(2,1)}, u32[]{:S(2)}) copy-start(bf16[1,3584,256]{2,1,0:T(8,128)(2,1)} %up_ref.1) | copy-start | bytes 5505028
  6.1 1.5 %copy-start.3 = (bf16[1,256,3584]{2,1,0:T(8,128)(2,1)S(1)}, bf16[1,256,3584]{2,1,0:T(8,128)(2,1)}, u32[]{:S(2)}) copy-start(bf16[1,256,3584]{2,1,0:T(8,128)(2,1)} %down_ref.1) | copy-start | bytes 5505028
  7.6 78.2 %copy-start.5 = (s32[4,17]{1,0:T(4,128)S(1)}, s32[4,17]{1,0:T(4,128)}, u32[]{:S(2)}) copy-start(s32[4,17]{1,0:T(4,128)} %table_ref.1) | copy-start | bytes 820
  7.6 78.2 %copy-start.7 = (s32[4]{0:T(128)S(1)}, s32[4]{0:T(128)}, u32[]{:S(2)}) copy-start(s32[4]{0:T(128)} %lengths_ref.1) | copy-start | bytes 52
  85.8 1.7 %copy-start = (bf16[32,288,128]{2,1,0:T(8,128)(2,1)S(1)}, bf16[32,288,128]{2,1,0:T(8,128)(2,1)}, u32[]{:S(2)}) copy-start(bf16[32,288,128]{2,1,0:T(8,128)(2,1)} %get-tuple-element.4.arrived_ref) | copy-start | bytes 7077892

commit v2 on v1

--- a/solution.py
+++ b/solution.py
@@ -16,6 +16,8 @@
 MESH = pl.DeviceIdType.MESH
 
 softmax_scale = 0.1353
+score_factor = softmax_scale * math.log2(math.e)
+W1, W2 = 4, 12
 
 
 def send(src, dst, send_sem, recv_sem, target):
@@ -48,8 +50,14 @@
     gate_ref,
     up_ref,
     down_ref,
+    table_ref,
+    lengths_ref,
+    queries_ref,
     arrived_ref,
     moe_ref,
+    rows_ref,
+    partial_ref,
+    stats_ref,
     pool_v,
     outgoing,
     gate_v,
@@ -62,6 +70,12 @@
     part_in,
     back_out,
     back_in,
+    queries_v,
+    rows_v,
+    keys,
+    bias,
+    partial_v,
+    stats_v,
     load_sem,
     mig_send,
     mig_recv,
@@ -73,6 +87,7 @@
     part_recv,
     back_send,
     back_recv,
+    store_sem,
 ):
     me = lax.axis_index("ep")
     planes = n // split
@@ -87,6 +102,7 @@
         pltpu.make_async_copy(gate_ref, gate_v, load_sem.at[1]),
         pltpu.make_async_copy(up_ref, up_v, load_sem.at[2]),
         pltpu.make_async_copy(down_ref, down_v, load_sem.at[3]),
+        pltpu.make_async_copy(queries_ref, queries_v, load_sem.at[4]),
     ]
     for load in loads:
         load.start()
@@ -128,14 +144,23 @@
 
     loads[0].wait()
 
+    def partner(k):
+        flips = n - (k * 11) % n
+        result = me
+        for bit in range(n.bit_length() - 1):
+            power = 2**bit
+            flip = (flips // power) % 2
+            held = (me // power) % 2
+            result = result + flip * (1 - 2 * held) * power
+        return result
+
     def mig_copy(k):
-        target = (me + k) % n
         return send(
-            outgoing.at[k], arrived_ref.at[me], mig_send.at[k], mig_recv.at[me], target
+            outgoing.at[k], arrived_ref.at[me], mig_send.at[k], mig_recv.at[me], partner(k)
         )
 
     def mig_start(k, carry):
-        target = (me + k) % n
+        target = partner(k)
         block = jnp.minimum(mig_ref[0, target], own_blocks - 1)
         for c in range(KVL // LANES):
             outgoing[k, c * 64 : (c + 1) * 64, :] = pool_v[
@@ -146,8 +171,50 @@
         mig_copy(k).start()
         return carry
 
-    far = n - split
-    lax.fori_loop(split, split + far // 2, mig_start, 0)
+    requests, blocks = table_ref.shape
+    positions = pool_ref.shape[1]
+    steps = queries_ref.shape[1]
+    heads = queries_ref.shape[3]
+
+    def kept_part(request, carry):
+        length = lengths_ref[request]
+        lane = lax.broadcasted_iota(jnp.int32, (1, positions), 1)
+        for b in range(blocks):
+            entry = table_ref[request, b]
+            span = slice(b * positions, (b + 1) * positions)
+            keys[span, :] = pool_v[jnp.minimum(entry, own_blocks - 1)]
+            limit = jnp.where(entry < own_blocks, length - b * positions, 0)
+            bias[:, span] = jnp.where(lane < limit, 0.0, -1e30)
+        for step in range(steps):
+            rows_v[request, step * heads : (step + 1) * heads, :] = queries_v[request, step].T
+        scores = (
+            lax.dot_general(
+                rows_v[request],
+                keys[...],
+                (((1,), (1,)), ((), ())),
+                preferred_element_type=jnp.float32,
+            )
+            * score_factor
+            + bias[...]
+        )
+        row_max = jnp.max(scores, axis=1, keepdims=True)
+        raised = jnp.exp2(scores - row_max)
+        total = jnp.sum(raised, axis=1, keepdims=True)
+        partial_v[request] = jnp.dot(
+            raised.astype(jnp.bfloat16), keys[:, :KVL], preferred_element_type=jnp.float32
+        )
+        lane = lax.broadcasted_iota(jnp.int32, (steps * heads, LANES), 1)
+        stats_v[request] = jnp.where(lane == 0, row_max, total)
+        return carry
+
+    stores = [
+        pltpu.make_async_copy(rows_v, rows_ref, store_sem.at[0]),
+        pltpu.make_async_copy(partial_v, partial_ref, store_sem.at[1]),
+        pltpu.make_async_copy(stats_v, stats_ref, store_sem.at[2]),
+    ]
+
+    first, second = 1 + (n - 1) * W1 // 31, 1 + (n - 1) * W2 // 31
+    lax.fori_loop(1, first, mig_start, 0)
 
     for k in range(1, planes):
         other = (plane + k) % planes
@@ -175,10 +242,11 @@
     for k in range(1, split):
         gather_copy(k).start()
 
-    lax.fori_loop(split + far // 2, n, mig_start, 0)
+    lax.fori_loop(first, second, mig_start, 0)
 
     for load in loads[1:]:
         load.wait()
+    lax.fori_loop(0, requests // 2, kept_part, 0)
     for k in range(1, split):
         other = (place + k) % split
         send(
@@ -215,7 +283,10 @@
         part_copy(k).start()
     part_in[place] = part_out[place]
 
-    lax.fori_loop(1, split, mig_start, 0)
+    lax.fori_loop(second, n, mig_start, 0)
+    lax.fori_loop(requests // 2, requests, kept_part, 0)
+    for store in stores:
+        store.start()
 
     for k in range(1, split):
         other = (place + k) % split
@@ -267,25 +338,45 @@
         part_copy(k).wait_send()
 
     def mig_wait(k, carry):
-        source = (me + k) % n
+        source = partner(k)
         send(
             outgoing.at[k], arrived_ref.at[source], mig_send.at[k], mig_recv.at[source], me
         ).wait_recv()
         mig_copy(k).wait_send()
         return carry
 
+    for store in stores:
+        store.wait()
     lax.fori_loop(1, n, mig_wait, 0)
 
 
-def exchange(cache_pool, mig_block, hidden_states, pick, combine, w_gate, w_up, w_down, n, split):
+def exchange(
+    cache_pool,
+    mig_block,
+    hidden_states,
+    pick,
+    combine,
+    w_gate,
+    w_up,
+    w_down,
+    block_table,
+    lengths,
+    queries,
+    n,
+    split,
+):
     blocks, positions, entries = cache_pool.shape
     tokens, model_width = hidden_states.shape
     packed = positions * entries // LANES
+    requests, steps, _, heads = queries.shape
+    height = steps * heads
+    length = block_table.shape[1] * positions
     planes = n // split
     chunk = planes * SLOT
     width = model_width // QUARTERS
     any_space = pl.BlockSpec(memory_space=pl.ANY)
     vmem = pl.BlockSpec(memory_space=pltpu.VMEM)
+    smem = pl.BlockSpec(memory_space=pltpu.SMEM)
     bf16 = jnp.bfloat16
     dma = pltpu.SemaphoreType.DMA
     return pl.pallas_call(
@@ -293,9 +384,12 @@
         out_shape=(
             jax.ShapeDtypeStruct((n, packed, LANES), bf16),
             jax.ShapeDtypeStruct((tokens, model_width), bf16),
+            jax.ShapeDtypeStruct((requests, height, entries), bf16),
+            jax.ShapeDtypeStruct((requests, height, KVL), jnp.float32),
+            jax.ShapeDtypeStruct((requests, height, LANES), jnp.float32),
         ),
         in_specs=[
-            pl.BlockSpec(memory_space=pltpu.SMEM),
+            smem,
             any_space,
             vmem,
             vmem,
@@ -303,8 +397,11 @@
             any_space,
             any_space,
             any_space,
+            smem,
+            smem,
+            any_space,
         ],
-        out_specs=(any_space, vmem),
+        out_specs=(any_space, vmem, any_space, any_space, any_space),
         scratch_shapes=[
             pltpu.VMEM(cache_pool.shape, bf16),
             pltpu.VMEM((n, packed, LANES), bf16),
@@ -318,7 +415,13 @@
             pltpu.VMEM((split, chunk, model_width), bf16),
             pltpu.VMEM((planes, SLOT * QUARTERS, width), bf16),
             pltpu.VMEM((planes, SLOT * QUARTERS, width), bf16),
-            dma((4,)),
+            pltpu.VMEM(queries.shape, bf16),
+            pltpu.VMEM((requests, height, entries), bf16),
+            pltpu.VMEM((length, entries), bf16),
+            pltpu.VMEM((1, length), jnp.float32),
+            pltpu.VMEM((requests, height, KVL), jnp.float32),
+            pltpu.VMEM((requests, height, LANES), jnp.float32),
+            dma((5,)),
             dma((n,)),
             dma((n,)),
             dma((planes,)),
@@ -329,98 +432,161 @@
             dma((split,)),
             dma((planes,)),
             dma((planes,)),
+            dma((3,)),
         ],
         compiler_params=pltpu.CompilerParams(
-            collective_id=0, has_side_effects=True, vmem_limit_bytes=48 * 1024 * 1024
+            collective_id=0, has_side_effects=True, vmem_limit_bytes=60 * 1024 * 1024
         ),
         name="exchange",
-    )(mig_block, cache_pool, hidden_states, pick, combine, w_gate, w_up, w_down)
-
-
-def attend_kernel(sizes, table_ref, lengths_ref, queries_ref, pool_ref, arrived_ref, out_ref, keys):
+    )(
+        mig_block,
+        cache_pool,
+        hidden_states,
+        pick,
+        combine,
+        w_gate,
+        w_up,
+        w_down,
+        block_table,
+        lengths,
+        queries,
+    )
+
+
+def attend_kernel(
+    own_blocks,
+    positions,
+    sizes,
+    table_ref,
+    lengths_ref,
+    rows_ref,
+    partial_ref,
+    stats_ref,
+    arrived_ref,
+    out_ref,
+    fetched,
+    keys,
+    sem,
+):
     request = pl.program_id(0)
-    own_blocks, positions, entries = pool_ref.shape
+    steps, heads = out_ref.shape[1], out_ref.shape[2]
     length = lengths_ref[request]
-    used = (length + positions - 1) // positions
+
+    def fetch(source):
+        return pltpu.make_async_copy(
+            arrived_ref.at[source], fetched.at[source], sem.at[source]
+        )
+
+    def used_blocks(row):
+        return (lengths_ref[row] + positions - 1) // positions
+
+    used = used_blocks(request)
 
     @pl.when(request == 0)
     def _():
+        for row in range(table_ref.shape[0]):
+
+            def begin(b, carry):
+                entry = table_ref[row, b]
+
+                @pl.when(entry >= own_blocks)
+                def _():
+                    fetch(entry - own_blocks).start()
+
+                return carry
+
+            lax.fori_loop(0, used_blocks(row), begin, 0)
         keys[...] = jnp.zeros_like(keys)
 
-    def place_block(b, carry):
+    def place_block(b, count):
         entry = table_ref[request, b]
-        start = pl.multiple_of(b * positions, positions)
-
-        @pl.when(entry < own_blocks)
-        def _():
-            keys[pl.ds(start, positions), :] = pool_ref[entry]
-
-        @pl.when(entry >= own_blocks)
+        moved = entry >= own_blocks
+
+        @pl.when(moved)
         def _():
             source = entry - own_blocks
+            fetch(source).wait()
+            start = pl.multiple_of(count * positions, positions)
+            half = positions // 2
             for c in range(KVL // LANES):
-                keys[pl.ds(start, positions), c * LANES : (c + 1) * LANES] = arrived_ref[
+                keys[pl.ds(start, positions), c * LANES : (c + 1) * LANES] = fetched[
                     source, c * positions : (c + 1) * positions, :
                 ]
-            tail = arrived_ref[source, 256:288, :]
-            keys[pl.ds(start, 32), KVL:] = tail[:, :64]
-            keys[pl.ds(start + 32, 32), KVL:] = tail[:, 64:]
-
-        return carry
-
-    lax.fori_loop(0, used, place_block, 0)
-    steps, heads = queries_ref.shape[1], queries_ref.shape[2]
-    queries = queries_ref[0].reshape(steps * heads, entries)
-
-    def attend(count):
-        rows = count * positions
-        scores = lax.dot_general(
-            queries,
-            keys[:rows, :],
-            (((1,), (1,)), ((), ())),
-            preferred_element_type=jnp.float32,
-        ) * (softmax_scale * math.log2(math.e))
+            tail = fetched[source, KVL // LANES * positions :, :]
+            keys[pl.ds(start, half), KVL:] = tail[:, :64]
+            keys[pl.ds(start + half, half), KVL:] = tail[:, 64:]
+
+        return count + moved.astype(jnp.int32)
+
+    count = lax.fori_loop(0, used, place_block, 0)
+    last_moved = table_ref[request, used - 1] >= own_blocks
+    limit = count * positions - jnp.where(last_moved, used * positions - length, 0)
+    old_max = stats_ref[0, :, 0:1]
+    old_total = stats_ref[0, :, 1:2]
+
+    @pl.when(count == 0)
+    def _():
+        out_ref[0] = (partial_ref[0] / old_total).astype(jnp.bfloat16).reshape(steps, heads, KVL)
+
+    def attend(size):
+        rows = size * positions
+        scores = (
+            lax.dot_general(
+                rows_ref[0],
+                keys[:rows, :],
+                (((1,), (1,)), ((), ())),
+                preferred_element_type=jnp.float32,
+            )
+            * score_factor
+        )
         where = lax.broadcasted_iota(jnp.int32, scores.shape, 1)
-        scores = jnp.where(where < length, scores, -1e30)
-        raised = jnp.exp2(scores - jnp.max(scores, axis=1, keepdims=True))
-        total = jnp.sum(raised, axis=1, keepdims=True)
-        out = jnp.dot(
+        scores = jnp.where(where < limit, scores, -1e30)
+        row_max = jnp.maximum(jnp.max(scores, axis=1, keepdims=True), old_max)
+        raised = jnp.exp2(scores - row_max)
+        keep = jnp.exp2(old_max - row_max)
+        total = jnp.sum(raised, axis=1, keepdims=True) + keep * old_total
+        out = keep * partial_ref[0] + jnp.dot(
             raised.astype(jnp.bfloat16), keys[:rows, :KVL], preferred_element_type=jnp.float32
         )
         out_ref[0] = (out / total).astype(jnp.bfloat16).reshape(steps, heads, KVL)
 
     low = 0
-    for count in sizes:
-
-        @pl.when((used > low) & (used <= count))
+    for size in sizes:
+
+        @pl.when((count > low) & (count <= size))
         def _():
-            attend(count)
-
-        low = count
-
-
-def attention(queries, cache_pool, arrived, block_table, lengths):
-    requests, steps, heads, entries = queries.shape
+            attend(size)
+
+        low = size
+
+
+def attention(block_table, lengths, rows, partial, stats, arrived, own_blocks, positions, steps):
+    requests, height, entries = rows.shape
     blocks = block_table.shape[1]
     sizes = tuple(c for c in (4, 8, 12) if c < blocks) + (blocks,)
     smem = pl.BlockSpec(memory_space=pltpu.SMEM)
-    vmem = pl.BlockSpec(memory_space=pltpu.VMEM)
+    heads = height // steps
     return pl.pallas_call(
-        functools.partial(attend_kernel, sizes),
+        functools.partial(attend_kernel, own_blocks, positions, sizes),
         grid=(requests,),
         out_shape=jax.ShapeDtypeStruct((requests, steps, heads, KVL), jnp.bfloat16),
         in_specs=[
             smem,
             smem,
-            pl.BlockSpec((1, steps, heads, entries), lambda r: (r, 0, 0, 0)),
-            vmem,
-            vmem,
+            pl.BlockSpec((1, height, entries), lambda r: (r, 0, 0)),
+            pl.BlockSpec((1, height, KVL), lambda r: (r, 0, 0)),
+            pl.BlockSpec((1, height, LANES), lambda r: (r, 0, 0)),
+            pl.BlockSpec(memory_space=pl.ANY),
         ],
         out_specs=pl.BlockSpec((1, steps, heads, KVL), lambda r: (r, 0, 0, 0)),
-        scratch_shapes=[pltpu.VMEM((blocks * cache_pool.shape[1], entries), jnp.bfloat16)],
-        compiler_params=pltpu.CompilerParams(vmem_limit_bytes=48 * 1024 * 1024),
+        scratch_shapes=[
+            pltpu.VMEM(arrived.shape, jnp.bfloat16),
+            pltpu.VMEM((blocks * positions, entries), jnp.bfloat16),
+            pltpu.SemaphoreType.DMA((arrived.shape[0],)),
+        ],
+        compiler_params=pltpu.CompilerParams(vmem_limit_bytes=60 * 1024 * 1024),
         name="attention",
-    )(block_table, lengths, queries, cache_pool, arrived)
+    )(block_table, lengths, rows, partial, stats, arrived)
 
 
 def local(
@@ -457,10 +623,32 @@
         both, weight[None, :, :, None, None], jnp.zeros((), jnp.bfloat16)
     ).reshape(QUARTERS, tokens, wide)
     pick = both.astype(jnp.bfloat16).reshape(QUARTERS, tokens, wide).swapaxes(1, 2)
-    arrived, moe_out = exchange(
-        cache_pool, mig_block, hidden_states, pick, combine, w_gate, w_up, w_down, n, split
+    arrived, moe_out, rows, partial, stats = exchange(
+        cache_pool,
+        mig_block,
+        hidden_states,
+        pick,
+        combine,
+        w_gate,
+        w_up,
+        w_down,
+        block_table,
+        lengths,
+        queries.swapaxes(2, 3),
+        n,
+        split,
     )
-    attn_out = attention(queries, cache_pool, arrived, block_table, lengths)
+    attn_out = attention(
+        block_table,
+        lengths,
+        rows,
+        partial,
+        stats,
+        arrived,
+        cache_pool.shape[0],
+        cache_pool.shape[1],
+        queries.shape[1],
+    )
     return attn_out, moe_out
 
 

time: 97.6 us -> 81.2 us (0.83)
  the two profiles are of different devices: /device:TPU:5 before, /device:TPU:0 now
where the time goes in v2:
time: 81.2 us; the launch traced here: 81.5 us
  Pallas kernels  77 us (95%)
  other arithmetic  2.92 us (4%)
  local copies, waits for them, and re-layouts  0.97 us (1%)
    pallas_call x1, Pallas kernels, exchange(): pl.pallas_call(functools.partial(exchange_kernel, n, split), out_shape=(j...  68.2 us
    pallas_call x1, Pallas kernels, attention(): pl.pallas_call(functools.partial(attend_kernel, own_blocks, positions, si...  8.73 us

profile of v2, /device:TPU:0, one launch (start us, length us, event | category | flops | bytes accessed | tf_op | source)
XLA Modules:
  0.0 81.5 jit_solution(1009453558011227333)
XLA Ops:
  0.6 0.7 fusion.2
  1.3 0.7 fusion.3
  2.0 0.2 convert_reduce_fusion
  2.2 0.1 copy.21
  2.3 0.1 and.61
  2.4 0.1 and.62
  2.5 0.1 copy.22
  2.6 0.6 and_select_fusion.combine_ref
  3.2 0.7 and_convert_fusion.pick_ref
  3.9 68.2 %exchange.1 = (bf16[32,288,128]{2,1,0:T(8,128)(2,1)}, bf16[8,3584]{1,0:T(8,128)(2,1)}, bf16[4,256,576]{2,1,0:T(8,128)(2,1)}, f32[4,256,512]{2,1,0:T(8,128)}, f32[4,256,128]{2,1,0:T(8,128)}) custom-call(s32[1,32]{1,0:T(1,128)} %mig_ref.1, bf16[68,64,576]{2,1,0:T(8,128)(2,1)} %pool_ref.1, bf16[8,3584]{1,0:T(8,128)(2,1)} %hidden_ref.1, ...), custom_call_target="tpu_custom_call" | custom-call | tf_op jit(solution)/shard_map/exchange/pallas_call | solution.py:382
  72.2 0.0 copy-start
  72.2 8.7 %attention.1 = bf16[4,2,128,512]{3,2,1,0:T(8,128)(2,1)} custom-call(s32[4,17]{1,0:T(4,128)} %table_ref.3, s32[4]{0:T(128)} %lengths_ref.3, bf16[4,256,576]{2,1,0:T(8,128)(2,1)} %get-tuple-element.7.rows_ref, f32[4,256,512]{2,1,0:T(8,128)} %get-tuple-element.8.partial_ref, f32[4,256,128]{2,1,0:T(8,128)} %get-tuple-element.9.stats_ref, ...), custom_call_target="tpu_custom_call" | custom-call | tf_op jit(solution)/shard_map/attention/pallas_call | solution.py:569
  80.9 0.0 copy-done
  80.9 0.6 copy.24
  (5 shorter events, 0.0 us)
Async XLA Ops:
  72.2 8.7 %copy-start = (bf16[8,3584]{1,0:T(8,128)(2,1)S(1)}, bf16[8,3584]{1,0:T(8,128)(2,1)}, u32[]{:S(2)}) copy-start(bf16[8,3584]{1,0:T(8,128)(2,1)} %get-tuple-element.15) | copy-start | bytes 172036

commit v3 on v2

--- a/solution.py
+++ b/solution.py
@@ -45,8 +45,8 @@
     mig_ref,
     pool_ref,
     hidden_ref,
-    pick_ref,
-    combine_ref,
+    routes_ref,
+    weight_ref,
     gate_ref,
     up_ref,
     down_ref,
@@ -97,6 +97,16 @@
     chunk = planes * SLOT
     wide = planes * SLOT * QUARTERS
 
+    barrier = pltpu.get_barrier_semaphore()
+
+    def greet(k, carry):
+        pl.semaphore_signal(
+            barrier, inc=1, device_id={"ep": (me + k) % n}, device_id_type=MESH
+        )
+        return carry
+
+    lax.fori_loop(1, n, greet, 0)
+
     loads = [
         pltpu.make_async_copy(pool_ref, pool_v, load_sem.at[0]),
         pltpu.make_async_copy(gate_ref, gate_v, load_sem.at[1]),
@@ -104,23 +114,37 @@
         pltpu.make_async_copy(down_ref, down_v, load_sem.at[3]),
         pltpu.make_async_copy(queries_ref, queries_v, load_sem.at[4]),
     ]
-    for load in loads:
-        load.start()
-
-    barrier = pltpu.get_barrier_semaphore()
-
-    def greet(k, carry):
-        pl.semaphore_signal(
-            barrier, inc=1, device_id={"ep": (me + k) % n}, device_id_type=MESH
-        )
-        return carry
-
-    lax.fori_loop(1, n, greet, 0)
+    loads[0].start()
+
+    tokens = hidden_ref.shape[0]
+    place_row = lax.broadcasted_iota(jnp.int32, (wide, tokens), 0)
+    expert, row_quarter, slot = place_row >> 4, (place_row >> 2) & 3, place_row & 3
+    hit = jnp.zeros((wide, tokens), jnp.float32)
+    weight = jnp.zeros((wide, tokens), jnp.float32)
+    weights = weight_ref[...].astype(jnp.float32)
+    for k in range(routes_ref.shape[0]):
+        same = routes_ref[k : k + 1, :] == expert
+        hit = jnp.where(same, 1.0, hit)
+        weight = jnp.where(same, weights[k : k + 1, :], weight)
+    earlier = jnp.where(
+        lax.broadcasted_iota(jnp.int32, (tokens, tokens), 0)
+        < lax.broadcasted_iota(jnp.int32, (tokens, tokens), 1),
+        1.0,
+        0.0,
+    )
+    rank = jnp.dot(
+        hit.astype(jnp.bfloat16), earlier.astype(jnp.bfloat16), preferred_element_type=jnp.float32
+    )
+    hit = jnp.where(rank == slot.astype(jnp.float32), hit, 0.0)
+    weight = weight * hit
+
+    def of_quarter(q, values):
+        return jnp.where(row_quarter == q, values, 0.0).astype(jnp.bfloat16)
 
     messages = jnp.zeros((wide, width), jnp.float32)
     for q in range(QUARTERS):
         messages += jnp.dot(
-            pick_ref[q],
+            of_quarter(q, hit),
             hidden_ref[:, q * width : (q + 1) * width],
             preferred_element_type=jnp.float32,
         )
@@ -143,6 +167,8 @@
         token_copy(k).start()
 
     loads[0].wait()
+    for load in loads[1:]:
+        load.start()
 
     def partner(k):
         flips = n - (k * 11) % n
@@ -326,8 +352,11 @@
         ).wait_recv()
     returned = back_in[...].reshape(wide, width)
     for q in range(QUARTERS):
-        moe_ref[:, q * width : (q + 1) * width] = jnp.dot(
-            combine_ref[q], returned, preferred_element_type=jnp.float32
+        moe_ref[:, q * width : (q + 1) * width] = lax.dot_general(
+            of_quarter(q, weight),
+            returned,
+            (((0,), (0,)), ((), ())),
+            preferred_element_type=jnp.float32,
         ).astype(jnp.bfloat16)
 
     for k in range(1, planes):
@@ -354,8 +383,8 @@
     cache_pool,
     mig_block,
     hidden_states,
-    pick,
-    combine,
+    routes,
+    route_weight,
     w_gate,
     w_up,
     w_down,
@@ -442,8 +471,8 @@
         mig_block,
         cache_pool,
         hidden_states,
-        pick,
-        combine,
+        routes,
+        route_weight,
         w_gate,
         w_up,
         w_down,
@@ -459,18 +488,25 @@
     sizes,
     table_ref,
     lengths_ref,
+    moe_ref,
     rows_ref,
     partial_ref,
     stats_ref,
     arrived_ref,
     out_ref,
+    moe_out_ref,
     fetched,
     keys,
+    rows_v,
+    partial_v,
+    stats_v,
+    out_v,
     sem,
+    load_sem,
+    store_sem,
 ):
-    request = pl.program_id(0)
-    steps, heads = out_ref.shape[1], out_ref.shape[2]
-    length = lengths_ref[request]
+    requests, steps, heads = out_v.shape[:3]
+    half = positions // 2
 
     def fetch(source):
         return pltpu.make_async_copy(
@@ -480,113 +516,144 @@
     def used_blocks(row):
         return (lengths_ref[row] + positions - 1) // positions
 
-    used = used_blocks(request)
-
-    @pl.when(request == 0)
-    def _():
-        for row in range(table_ref.shape[0]):
-
-            def begin(b, carry):
-                entry = table_ref[row, b]
-
-                @pl.when(entry >= own_blocks)
-                def _():
-                    fetch(entry - own_blocks).start()
-
-                return carry
-
-            lax.fori_loop(0, used_blocks(row), begin, 0)
-        keys[...] = jnp.zeros_like(keys)
-
-    def place_block(b, count):
-        entry = table_ref[request, b]
-        moved = entry >= own_blocks
-
-        @pl.when(moved)
+    def begin(row):
+        def begin_block(b, carry):
+            entry = table_ref[row, b]
+
+            @pl.when(entry >= own_blocks)
+            def _():
+                fetch(entry - own_blocks).start()
+
+            return carry
+
+        lax.fori_loop(0, used_blocks(row), begin_block, 0)
+
+    def load_parts(row):
+        return [
+            pltpu.make_async_copy(whole.at[row], held.at[row], load_sem.at[part, row])
+            for part, (whole, held) in enumerate(
+                ((rows_ref, rows_v), (stats_ref, stats_v), (partial_ref, partial_v))
+            )
+        ]
+
+    def store_part(row):
+        return pltpu.make_async_copy(out_v.at[row], out_ref.at[row], store_sem.at[row])
+
+    for row in range(requests):
+        begin(row)
+        for load in load_parts(row):
+            load.start()
+    keys[...] = jnp.zeros_like(keys)
+    moe_out_ref[...] = moe_ref[...]
+
+    def one_request(request, carry):
+        length = lengths_ref[request]
+        used = used_blocks(request)
+
+        def place_block(b, count):
+            entry = table_ref[request, b]
+            moved = entry >= own_blocks
+
+            @pl.when(moved)
+            def _():
+                source = entry - own_blocks
+                fetch(source).wait()
+                start = pl.multiple_of(count * positions, positions)
+                for c in range(KVL // LANES):
+                    keys[pl.ds(start, positions), c * LANES : (c + 1) * LANES] = fetched[
+                        source, c * positions : (c + 1) * positions, :
+                    ]
+                tail = fetched[source, KVL // LANES * positions :, :]
+                keys[pl.ds(start, half), KVL:] = tail[:, :64]
+                keys[pl.ds(start + half, half), KVL:] = tail[:, 64:]
+
+            return count + moved.astype(jnp.int32)
+
+        count = lax.fori_loop(0, used, place_block, 0)
+        last_moved = table_ref[request, used - 1] >= own_blocks
+        limit = count * positions - jnp.where(last_moved, used * positions - length, 0)
+        for load in load_parts(request):
+            load.wait()
+        old_max = stats_v[request, :, 0:1]
+        old_total = stats_v[request, :, 1:2]
+
+        def finish(out, total):
+            out_v[request] = (
+                (out * (1.0 / total)).astype(jnp.bfloat16).reshape(steps, heads, KVL)
+            )
+
+        @pl.when(count == 0)
         def _():
-            source = entry - own_blocks
-            fetch(source).wait()
-            start = pl.multiple_of(count * positions, positions)
-            half = positions // 2
-            for c in range(KVL // LANES):
-                keys[pl.ds(start, positions), c * LANES : (c + 1) * LANES] = fetched[
-                    source, c * positions : (c + 1) * positions, :
-                ]
-            tail = fetched[source, KVL // LANES * positions :, :]
-            keys[pl.ds(start, half), KVL:] = tail[:, :64]
-            keys[pl.ds(start + half, half), KVL:] = tail[:, 64:]
-
-        return count + moved.astype(jnp.int32)
-
-    count = lax.fori_loop(0, used, place_block, 0)
-    last_moved = table_ref[request, used - 1] >= own_blocks
-    limit = count * positions - jnp.where(last_moved, used * positions - length, 0)
-    old_max = stats_ref[0, :, 0:1]
-    old_total = stats_ref[0, :, 1:2]
-
-    @pl.when(count == 0)
-    def _():
-        out_ref[0] = (partial_ref[0] / old_total).astype(jnp.bfloat16).reshape(steps, heads, KVL)
-
-    def attend(size):
-        rows = size * positions
-        scores = (
-            lax.dot_general(
-                rows_ref[0],
-                keys[:rows, :],
-                (((1,), (1,)), ((), ())),
+            finish(partial_v[request], old_total)
+
+        def attend(size):
+            rows = size * positions
+            scores = (
+                lax.dot_general(
+                    rows_v[request],
+                    keys[:rows, :],
+                    (((1,), (1,)), ((), ())),
+                    preferred_element_type=jnp.float32,
+                )
+                * score_factor
+            )
+            where = lax.broadcasted_iota(jnp.int32, scores.shape, 1)
+            scores = jnp.where(where < limit, scores, -1e30)
+            row_max = jnp.maximum(jnp.max(scores, axis=1, keepdims=True), old_max)
+            raised = jnp.exp2(scores - row_max)
+            keep = jnp.exp2(old_max - row_max)
+            total = jnp.sum(raised, axis=1, keepdims=True) + keep * old_total
+            out = keep * partial_v[request] + jnp.dot(
+                raised.astype(jnp.bfloat16),
+                keys[:rows, :KVL],
                 preferred_element_type=jnp.float32,
             )
-            * score_factor
-        )
-        where = lax.broadcasted_iota(jnp.int32, scores.shape, 1)
-        scores = jnp.where(where < limit, scores, -1e30)
-        row_max = jnp.maximum(jnp.max(scores, axis=1, keepdims=True), old_max)
-        raised = jnp.exp2(scores - row_max)
-        keep = jnp.exp2(old_max - row_max)
-        total = jnp.sum(raised, axis=1, keepdims=True) + keep * old_total
-        out = keep * partial_ref[0] + jnp.dot(
-            raised.astype(jnp.bfloat16), keys[:rows, :KVL], preferred_element_type=jnp.float32
-        )
-        out_ref[0] = (out / total).astype(jnp.bfloat16).reshape(steps, heads, KVL)
-
-    low = 0
-    for size in sizes:
-
-        @pl.when((count > low) & (count <= size))
-        def _():
-            attend(size)
-
-        low = size
-
-
-def attention(block_table, lengths, rows, partial, stats, arrived, own_blocks, positions, steps):
+            finish(out, total)
+
+        low = 0
+        for size in sizes:
+
+            @pl.when((count > low) & (count <= size))
+            def _():
+                attend(size)
+
+            low = size
+        store_part(request).start()
+        return carry
+
+    lax.fori_loop(0, requests, one_request, 0)
+    for row in range(requests):
+        store_part(row).wait()
+
+
+def attention(block_table, lengths, moe, rows, partial, stats, arrived, own_blocks, positions, steps):
     requests, height, entries = rows.shape
     blocks = block_table.shape[1]
-    sizes = tuple(c for c in (4, 8, 12) if c < blocks) + (blocks,)
+    sizes = tuple(c for c in (2, 4, 6, 8, 12) if c < blocks) + (blocks,)
     smem = pl.BlockSpec(memory_space=pltpu.SMEM)
+    vmem = pl.BlockSpec(memory_space=pltpu.VMEM)
+    any_space = pl.BlockSpec(memory_space=pl.ANY)
     heads = height // steps
+    out_shape = jax.ShapeDtypeStruct((requests, steps, heads, KVL), jnp.bfloat16)
     return pl.pallas_call(
         functools.partial(attend_kernel, own_blocks, positions, sizes),
-        grid=(requests,),
-        out_shape=jax.ShapeDtypeStruct((requests, steps, heads, KVL), jnp.bfloat16),
-        in_specs=[
-            smem,
-            smem,
-            pl.BlockSpec((1, height, entries), lambda r: (r, 0, 0)),
-            pl.BlockSpec((1, height, KVL), lambda r: (r, 0, 0)),
-            pl.BlockSpec((1, height, LANES), lambda r: (r, 0, 0)),
-            pl.BlockSpec(memory_space=pl.ANY),
-        ],
-        out_specs=pl.BlockSpec((1, steps, heads, KVL), lambda r: (r, 0, 0, 0)),
+        out_shape=(out_shape, jax.ShapeDtypeStruct(moe.shape, moe.dtype)),
+        in_specs=[smem, smem, vmem, any_space, any_space, any_space, any_space],
+        out_specs=(any_space, vmem),
         scratch_shapes=[
             pltpu.VMEM(arrived.shape, jnp.bfloat16),
             pltpu.VMEM((blocks * positions, entries), jnp.bfloat16),
+            pltpu.VMEM(rows.shape, rows.dtype),
+            pltpu.VMEM(partial.shape, partial.dtype),
+            pltpu.VMEM(stats.shape, stats.dtype),
+            pltpu.VMEM(out_shape.shape, out_shape.dtype),
             pltpu.SemaphoreType.DMA((arrived.shape[0],)),
+            pltpu.SemaphoreType.DMA((3, requests)),
+            pltpu.SemaphoreType.DMA((requests,)),
         ],
         compiler_params=pltpu.CompilerParams(vmem_limit_bytes=60 * 1024 * 1024),
         name="attention",
-    )(block_table, lengths, rows, partial, stats, arrived)
+    )(block_table, lengths, moe, rows, partial, stats, arrived)
 
 
 def local(
@@ -604,31 +671,12 @@
 ):
     n = lax.axis_size("ep")
     split = FF // w_gate.shape[2]
-    experts = n // split
-    tokens = hidden_states.shape[0]
-    ids = jnp.arange(experts, dtype=jnp.int32)
-    matches = routes[:, :, None] == ids[None, None, :]
-    hit = jnp.any(matches, axis=1)
-    weight = jnp.sum(jnp.where(matches, route_weight[:, :, None], jnp.zeros((), jnp.bfloat16)), axis=1)
-    order = jnp.arange(tokens)
-    earlier = order[None, :] < order[:, None]
-    rank = jnp.sum((earlier[:, :, None] & hit[None, :, :]).astype(jnp.int32), axis=1)
-    slots = jnp.arange(SLOT)
-    chosen = hit[:, :, None] & (rank[:, :, None] == slots)
-    quarters = jnp.arange(QUARTERS)
-    same = quarters[:, None] == quarters[None, :]
-    wide = experts * QUARTERS * SLOT
-    both = same[:, None, None, :, None] & chosen[None, :, :, None, :]
-    combine = jnp.where(
-        both, weight[None, :, :, None, None], jnp.zeros((), jnp.bfloat16)
-    ).reshape(QUARTERS, tokens, wide)
-    pick = both.astype(jnp.bfloat16).reshape(QUARTERS, tokens, wide).swapaxes(1, 2)
     arrived, moe_out, rows, partial, stats = exchange(
         cache_pool,
         mig_block,
         hidden_states,
-        pick,
-        combine,
+        routes.T,
+        route_weight.T,
         w_gate,
         w_up,
         w_down,
@@ -638,9 +686,10 @@
         n,
         split,
     )
-    attn_out = attention(
+    return attention(
         block_table,
         lengths,
+        moe_out,
         rows,
         partial,
         stats,
@@ -649,7 +698,6 @@
         cache_pool.shape[1],
         queries.shape[1],
     )
-    return attn_out, moe_out
 
 
 def solution(mesh):

time: 81.2 us -> 77.3 us (0.952)
  other arithmetic: 2.92 us -> 0 us
  local copies, waits for them, and re-layouts: 0.97 us -> 0 us
    reduce_sum x2 -> x0, other arithmetic: 0.85 us -> none  [the longest x1 0.69 us: local(): jnp.sum(jnp.where(matches, route_weight[:, :, None], jnp.zeros((), jnp.bf...]
where the time goes in v3:
time: 77.3 us; the launch traced here: 76.8 us
  Pallas kernels  76.2 us (99%)
    pallas_call x1, Pallas kernels, exchange(): pl.pallas_call(functools.partial(exchange_kernel, n, split), out_shape=(j...  68.2 us
    pallas_call x1, Pallas kernels, attention(): pl.pallas_call(functools.partial(attend_kernel, own_blocks, positions, si...  7.96 us

profile of v3, /device:TPU:0, one launch (start us, length us, event | category | flops | bytes accessed | tf_op | source)
XLA Modules:
  0.0 76.8 jit_solution(12954877702916027182)
XLA Ops:
  0.6 68.2 %exchange.1 = (bf16[32,288,128]{2,1,0:T(8,128)(2,1)}, bf16[8,3584]{1,0:T(8,128)(2,1)}, bf16[4,256,576]{2,1,0:T(8,128)(2,1)}, f32[4,256,512]{2,1,0:T(8,128)}, f32[4,256,128]{2,1,0:T(8,128)}) custom-call(s32[1,32]{1,0:T(1,128)} %mig_ref.1, bf16[68,64,576]{2,1,0:T(8,128)(2,1)} %pool_ref.1, bf16[8,3584]{1,0:T(8,128)(2,1)} %hidden_ref.1, s32[2,8]{1,0:T(2,128)} %bitcast.4, ...), custom_call_target="tpu_custom_call" | custom-call | tf_op jit(solution)/shard_map/exchange/pallas_call | solution.py:411
  68.9 8.0 %attention.1 = (bf16[4,2,128,512]{3,2,1,0:T(8,128)(2,1)}, bf16[8,3584]{1,0:T(8,128)(2,1)}) custom-call(s32[4,17]{1,0:T(4,128)} %table_ref.3, s32[4]{0:T(128)} %lengths_ref.3, bf16[8,3584]{1,0:T(8,128)(2,1)} %get-tuple-element.7.moe_ref, bf16[4,256,576]{2,1,0:T(8,128)(2,1)} %get-tuple-element.8.rows_ref, f32[4,256,512]{2,1,0:T(8,128)} %get-tuple-element.9.partial_ref, ...), custom_call_target="tpu_custom_call" | custom-call | tf_op jit(solution)/shard_map/attention/pallas_call | solution.py:638

commit v4 on v3

--- a/solution.py
+++ b/solution.py
@@ -108,13 +108,20 @@
     lax.fori_loop(1, n, greet, 0)
 
     loads = [
-        pltpu.make_async_copy(pool_ref, pool_v, load_sem.at[0]),
         pltpu.make_async_copy(gate_ref, gate_v, load_sem.at[1]),
         pltpu.make_async_copy(up_ref, up_v, load_sem.at[2]),
         pltpu.make_async_copy(down_ref, down_v, load_sem.at[3]),
         pltpu.make_async_copy(queries_ref, queries_v, load_sem.at[4]),
     ]
-    loads[0].start()
+    part = own_blocks // 4
+    pool_loads = [
+        pltpu.make_async_copy(
+            pool_ref.at[pl.ds(c * part, part)], pool_v.at[pl.ds(c * part, part)], load_sem.at[5 + c]
+        )
+        for c in range(4)
+    ]
+    for load in pool_loads:
+        load.start()
 
     tokens = hidden_ref.shape[0]
     place_row = lax.broadcasted_iota(jnp.int32, (wide, tokens), 0)
@@ -166,8 +173,9 @@
     for k in range(1, planes):
         token_copy(k).start()
 
-    loads[0].wait()
-    for load in loads[1:]:
+    for load in pool_loads:
+        load.wait()
+    for load in loads:
         load.start()
 
     def partner(k):
@@ -270,7 +278,7 @@
 
     lax.fori_loop(first, second, mig_start, 0)
 
-    for load in loads[1:]:
+    for load in loads:
         load.wait()
     lax.fori_loop(0, requests // 2, kept_part, 0)
     for k in range(1, split):
@@ -450,7 +458,7 @@
             pltpu.VMEM((1, length), jnp.float32),
             pltpu.VMEM((requests, height, KVL), jnp.float32),
             pltpu.VMEM((requests, height, LANES), jnp.float32),
-            dma((5,)),
+            dma((9,)),
             dma((n,)),
             dma((n,)),
             dma((planes,)),

time: 77.3 us -> 78.4 us (1.014)
  Pallas kernels: 76.2 us -> 77.4 us
    pallas_call x1, Pallas kernels: 7.96 us -> 9.11 us  [attention(): pl.pallas_call(functools.partial(attend_kernel, own_blocks, positions, si...]
where the time goes in v4:
time: 78.4 us; the launch traced here: 78 us
  Pallas kernels  77.4 us (99%)
    pallas_call x1, Pallas kernels, exchange(): pl.pallas_call(functools.partial(exchange_kernel, n, split), out_shape=(j...  68.3 us
    pallas_call x1, Pallas kernels, attention(): pl.pallas_call(functools.partial(attend_kernel, own_blocks, positions, si...  9.11 us

profile of v4, /device:TPU:0, one launch (start us, length us, event | category | flops | bytes accessed | tf_op | source)
XLA Modules:
  0.0 78.0 jit_solution(18073049701432543373)
XLA Ops:
  0.6 68.3 %exchange.1 = (bf16[32,288,128]{2,1,0:T(8,128)(2,1)}, bf16[8,3584]{1,0:T(8,128)(2,1)}, bf16[4,256,576]{2,1,0:T(8,128)(2,1)}, f32[4,256,512]{2,1,0:T(8,128)}, f32[4,256,128]{2,1,0:T(8,128)}) custom-call(s32[1,32]{1,0:T(1,128)} %mig_ref.1, bf16[68,64,576]{2,1,0:T(8,128)(2,1)} %pool_ref.1, bf16[8,3584]{1,0:T(8,128)(2,1)} %hidden_ref.1, s32[2,8]{1,0:T(2,128)} %bitcast.4, ...), custom_call_target="tpu_custom_call" | custom-call | tf_op jit(solution)/shard_map/exchange/pallas_call | solution.py:419
  68.9 9.1 %attention.1 = (bf16[4,2,128,512]{3,2,1,0:T(8,128)(2,1)}, bf16[8,3584]{1,0:T(8,128)(2,1)}) custom-call(s32[4,17]{1,0:T(4,128)} %table_ref.3, s32[4]{0:T(128)} %lengths_ref.3, bf16[8,3584]{1,0:T(8,128)(2,1)} %get-tuple-element.7.moe_ref, bf16[4,256,576]{2,1,0:T(8,128)(2,1)} %get-tuple-element.8.rows_ref, f32[4,256,512]{2,1,0:T(8,128)} %get-tuple-element.9.partial_ref, ...), custom_call_target="tpu_custom_call" | custom-call | tf_op jit(solution)/shard_map/attention/pallas_call | solution.py:646
